TPU v7x, 32 devices: a whole 2x2x4 slice. The times are simulated.
32 devices in a mesh: blocks: 2 (over y), tile: 16 (over z, x, core).
Axes of the slice: x: 2, y: 2, z: 4, core: 2. Of those that a mesh axis runs over, the one named last changes fastest.
Arguments:
- raw_views: bfloat16 [8, 1024, 32, 128], P(None, ('blocks', 'tile')), parts along dimension 1, as said below
- spread_taps: float32 [8, 2, 3, 31], replicated, may hold values from 0.0001 to 1, as said below
Outputs:
- estimate: float32 [1024, 32, 128], P(('blocks', 'tile')), parts along dimension 0
There are 2 independent parts, one for each index of `blocks`. A program takes and returns all parts, laid end to end along the dimension named above; an argument that names none is the same for every part. Nothing has to cross between parts.
Inputs may be any that keep to these rules, and one draw needn't show every extreme that they name: `raw_views`: every entry is positive. `spread_taps`: every tap is positive.
All inputs are finite; a program needn't handle non-finite values.
Results may differ from a plain program's by a relative error of at most 0.0031.
Values may be sent and summed in bfloat16 or wider, within the bound.
A program may use at most 64 MiB of HBM per device.

v0:
```python
import functools

import jax
import jax.numpy as jnp
from jax import lax
from jax.experimental import pallas as pl
from jax.experimental.pallas import tpu as pltpu
from jax.sharding import PartitionSpec as P

ITERS = 2
SUB = 8
HALO = 16
F32 = jnp.float32
BF16 = jnp.bfloat16
MESH = pl.DeviceIdType.MESH


def dot(a, b):
    return jnp.dot(a, b, preferred_element_type=F32)


def kernel_body(
    n, radius, raw_in, taps, out, relay, raw, esto, estp, estn, est, fac, zin, qx,
    wxf, wxb, ykf, ykb, zf, zb, brow, tot, scl,
    tot_ss, tot_rs, raw_ss, raw_rs, est_ss, est_rs,
):
    views, planes, height, width = raw_in.shape
    terms = zb.shape[1] // planes
    me = lax.axis_index("tile")
    prev, nxt = lax.rem(me + n - 1, n), lax.rem(me + 1, n)
    has_prev, has_next = me > 0, me < n - 1
    groups = planes // SUB
    own = planes // HALO
    wide = own + 2

    barrier = pltpu.get_barrier_semaphore()

    def greet(i, c):
        pl.semaphore_signal(
            barrier, inc=1, device_id={"tile": lax.rem(me + i, n)}, device_id_type=MESH
        )
        return c

    lax.fori_loop(1, n, greet, 0)

    def relayout(v, c):
        for z in range(planes):
            relay[pl.ds(z, height, stride=planes), :] = raw_in[v, z].astype(F32)
        block = relay[...].reshape(height, planes, width)
        for k in range(own):
            raw[v, 1 + k] = block[:, k * HALO:(k + 1) * HALO, :].astype(BF16)
        tot[0, pl.ds(v, 1), :] = jnp.sum(relay[...], axis=0, keepdims=True)
        return c

    lax.fori_loop(0, views, relayout, 0)
    pl.semaphore_wait(barrier, n - 1)

    def tot_copy(i):
        return pltpu.make_async_remote_copy(
            src_ref=tot.at[0], dst_ref=tot.at[i], send_sem=tot_ss.at[i], recv_sem=tot_rs.at[i],
            device_id={"tile": lax.rem(me + i, n)}, device_id_type=MESH,
        )

    def tot_start(i, c):
        tot_copy(i).start()
        return c

    def tot_wait(i, c):
        tot_copy(i).wait()
        return c

    lax.fori_loop(1, n, tot_start, 0)

    def exchange(src_lo, dst_lo, src_hi, dst_hi, ss, rs):
        down = pltpu.make_async_remote_copy(
            src_ref=src_lo, dst_ref=dst_hi, send_sem=ss.at[0], recv_sem=rs.at[0],
            device_id={"tile": prev}, device_id_type=MESH,
        )
        up = pltpu.make_async_remote_copy(
            src_ref=src_hi, dst_ref=dst_lo, send_sem=ss.at[1], recv_sem=rs.at[1],
            device_id={"tile": nxt}, device_id_type=MESH,
        )

        def start():
            @pl.when(has_prev)
            def _():
                down.start()

            @pl.when(has_next)
            def _():
                up.start()

        def wait_recv():
            @pl.when(has_prev)
            def _():
                up.wait_recv()

            @pl.when(has_next)
            def _():
                down.wait_recv()

        def wait_send():
            @pl.when(has_prev)
            def _():
                down.wait_send()

            @pl.when(has_next)
            def _():
                up.wait_send()

        return start, wait_recv, wait_send

    raw_x = exchange(
        raw.at[:, 1], raw.at[:, 0], raw.at[:, own], raw.at[:, own + 1], raw_ss, raw_rs
    )
    est_x = [
        exchange(
            esto.at[i], estp.at[i], esto.at[i], estn.at[i], est_ss.at[i], est_rs.at[i]
        )
        for i in range(ITERS)
    ]
    raw_x[0]()

    @pl.when(me == 0)
    def _():
        estp[...] = jnp.zeros_like(estp)
        raw[:, 0] = jnp.zeros_like(raw[:, 0])

    @pl.when(me == n - 1)
    def _():
        estn[...] = jnp.zeros_like(estn)
        raw[:, own + 1] = jnp.zeros_like(raw[:, own + 1])

    lanes = taps.shape[1]
    tap = lax.broadcasted_iota(jnp.int32, (lanes, lanes), 0)
    lane = lax.broadcasted_iota(jnp.int32, (lanes, lanes), 1)
    signed = jnp.where(lane < lanes // 2, lane, lane - lanes)
    far = lane - lanes
    vt = views * terms

    def place(k, dim, wanted, keep=None):
        hit = tap == wanted
        if keep is not None:
            hit = jnp.logical_and(hit, keep)
        brow[k] = dot(taps[dim * vt:(dim + 1) * vt, :], hit.astype(F32).astype(BF16))

    step = lane % SUB == 0
    place(0, 2, radius - signed)
    place(1, 2, radius + signed)
    place(2, 1, lane // SUB + radius, step)
    place(3, 1, lane // SUB + radius - lanes // SUB, step)
    place(4, 1, radius - lane // SUB, step)
    place(5, 1, radius - lane // SUB + lanes // SUB, step)
    place(6, 0, lane - (HALO - radius))
    place(7, 0, 2 * radius + HALO - radius - lane)

    row = tap
    near = jnp.abs(row - lane) <= radius
    after = lane >= row

    def rolled(k, i, rows):
        line = jnp.broadcast_to(brow[k, pl.ds(i, 1), :], (rows, lanes))
        return pltpu.roll(line, 0, 1, stride=1, stride_axis=0)

    def tables(wx, yk, z, kx, ky, kz, zrows, zcols):
        def one(v, c):
            for t in range(terms):
                i = v * terms + t
                wx[v, t * width:(t + 1) * width, :] = jnp.where(
                    near, rolled(kx, i, width), 0.0
                ).astype(BF16)
                r0 = rolled(ky, i, lanes)
                r1 = rolled(ky + 1, i, lanes)
                t0 = jnp.where(after, r0, r1).astype(BF16)
                yk[i, 0:lanes, 0:lanes] = t0
                yk[i, lanes:2 * lanes, lanes:2 * lanes] = t0
                yk[i, 0:lanes, lanes:2 * lanes] = jnp.where(after, 0.0, r0).astype(BF16)
                yk[i, lanes:2 * lanes, 0:lanes] = jnp.where(after, r1, 0.0).astype(BF16)
                z[v, t * zrows:(t + 1) * zrows, :] = rolled(kz, i, zrows)[:, :zcols].astype(BF16)
            return c

        lax.fori_loop(0, views, one, 0)

    tables(wxf, ykf, zf, 0, 2, 6, wide * HALO, zf.shape[2])

    lax.fori_loop(1, n, tot_wait, 0)
    summed = lax.fori_loop(0, n, lambda i, a: a + tot[i], jnp.zeros(tot.shape[1:], F32))
    totals = jnp.sum(summed, axis=1, keepdims=True)
    mean = jnp.sum(totals, axis=0, keepdims=True) / views
    scl[...] = jnp.broadcast_to(mean / totals, scl.shape)

    chunk = SUB
    for k in range(own):
        def first(j, c):
            acc = jnp.zeros((chunk, HALO, width), F32)
            for v in range(views):
                s = scl[v:v + 1, :].reshape(1, 1, width)
                acc = acc + s * raw[v, 1 + k, pl.ds(j * chunk, chunk)].astype(F32)
            acc = acc / views
            for h in range(HALO // SUB):
                est[k * (HALO // SUB) + h, pl.ds(j * chunk * SUB, chunk * SUB), :] = acc[
                    :, h * SUB:(h + 1) * SUB, :
                ].reshape(chunk * SUB, width)
            esto[0, pl.ds(j * chunk, chunk), k * HALO:(k + 1) * HALO, :] = acc.astype(BF16)
            return c

        lax.fori_loop(0, height // chunk, first, 0)

    est_x[0][0]()
    tables(wxb, ykb, zb, 1, 4, 7, planes, zb.shape[2])

    pairs = height // 2
    fgroups = wide * HALO // SUB

    def yx(yk, wx, v, base, gcount, gp):
        ys = []
        for t in range(terms):
            i = base + t * gcount + 2 * gp
            rhs = jnp.concatenate([zin[i], zin[i + 1]], axis=1)
            ys.append(dot(yk[v * terms + t], rhs).astype(BF16))
        res = []
        for h in range(2):
            lhs = jnp.concatenate([y[:, h * width:(h + 1) * width] for y in ys], axis=1)
            res.append(dot(lhs, wx[v]))
        return res

    for it in range(ITERS):
        est_x[it][1]()

        def zforward(p, c):
            cols = []
            for h in range(2):
                y = 2 * p + h
                cols.append(jnp.concatenate([estp[it, y], esto[it, y], estn[it, y]], axis=0))
            rhs = jnp.concatenate(cols, axis=1)
            r = dot(zf[...].reshape(-1, zf.shape[2]), rhs)
            r = r.reshape(vt * fgroups, SUB, 2 * width)
            r = jnp.concatenate([r[:, :, :width], r[:, :, width:]], axis=1)
            zin[:, pl.ds(pl.multiple_of(p * 2 * SUB, 2 * SUB), 2 * SUB), :] = r.astype(BF16)
            return c

        lax.fori_loop(0, pairs, zforward, 0)

        def forward(gps):
            def one(v, c):
                s = scl[pl.ds(v, 1), :].reshape(1, 1, width)
                for gp in gps:
                    res = yx(ykf, wxf, v, v * terms * fgroups, fgroups, gp)
                    b = jnp.concatenate([x.reshape(height, SUB, width) for x in res], axis=1)
                    q = s * raw[v, gp].astype(F32) / b
                    if gp == 0:
                        q = jnp.where(has_prev, q, 0.0)
                    if gp == wide - 1:
                        q = jnp.where(has_next, q, 0.0)
                    qx[v, gp] = q.astype(BF16)
                return c

            lax.fori_loop(0, views, one, 0)

        forward(range(1, wide - 1))
        if it == 0:
            raw_x[1]()
        forward((0, wide - 1))

        def zbackward(v, c):
            for p in range(pairs):
                cols = [
                    jnp.concatenate([qx[v, g, 2 * p + h] for g in range(wide)], axis=0)
                    for h in range(2)
                ]
                r = dot(zb[v], jnp.concatenate(cols, axis=1))
                r = r.reshape(terms * groups, SUB, 2 * width)
                r = jnp.concatenate([r[:, :, :width], r[:, :, width:]], axis=1)
                zin[pl.ds(v * terms * groups, terms * groups), p * 2 * SUB:(p + 1) * 2 * SUB, :] = (
                    r.astype(BF16)
                )
            return c

        lax.fori_loop(0, views, zbackward, 0)
        fac[...] = jnp.ones_like(fac)

        def backward(v, c):
            for gp in range(own):
                res = yx(ykb, wxb, v, v * terms * groups, groups, gp)
                for h in range(2):
                    fac[2 * gp + h] = fac[2 * gp + h] * res[h]
            return c

        lax.fori_loop(0, views, backward, 0)

        for k in range(own):
            parts = []
            for h in range(2):
                g = 2 * k + h
                new = est[g] * fac[g]
                est[g] = new
                parts.append(new.reshape(height, SUB, width))
            if it + 1 < ITERS:
                esto[it + 1, :, k * HALO:(k + 1) * HALO, :] = jnp.concatenate(
                    parts, axis=1
                ).astype(BF16)
        if it + 1 < ITERS:
            est_x[it + 1][0]()

    for g in range(groups):
        for z in range(SUB):
            out[g * SUB + z] = est[g, pl.ds(z, height, stride=SUB), :]

    raw_x[2]()
    for it in range(ITERS):
        est_x[it][2]()


def local(n, raw_views, spread_taps):
    views, planes, height, width = raw_views.shape
    terms, tap_count = spread_taps.shape[1], spread_taps.shape[3]
    radius = (tap_count - 1) // 2
    vt = views * terms
    taps = spread_taps.astype(BF16).transpose(2, 0, 1, 3).reshape(3 * vt, tap_count)
    taps = jnp.pad(taps, ((0, 0), (0, width - tap_count)))
    own = planes // HALO
    wide = own + 2
    area = SUB * height
    slab = (ITERS, height, planes, width)
    scratch = [
        pltpu.VMEM((planes * height, width), F32),
        pltpu.VMEM((views, wide, height, HALO, width), BF16),
        pltpu.VMEM(slab, BF16),
        pltpu.VMEM(slab, BF16),
        pltpu.VMEM(slab, BF16),
        pltpu.VMEM((planes // SUB, area, width), F32),
        pltpu.VMEM((planes // SUB, area, width), F32),
        pltpu.VMEM((vt * wide * HALO // SUB, area, width), BF16),
        pltpu.VMEM((views, wide, height, HALO, width), BF16),
        pltpu.VMEM((views, terms * width, width), BF16),
        pltpu.VMEM((views, terms * width, width), BF16),
        pltpu.VMEM((vt, area, area), BF16),
        pltpu.VMEM((vt, area, area), BF16),
        pltpu.VMEM((views, terms * wide * HALO, 3 * planes), BF16),
        pltpu.VMEM((views, terms * planes, wide * HALO), BF16),
        pltpu.VMEM((8, vt, width), F32),
        pltpu.VMEM((n, views, width), F32),
        pltpu.VMEM((views, width), F32),
        pltpu.SemaphoreType.DMA((n,)),
        pltpu.SemaphoreType.DMA((n,)),
        pltpu.SemaphoreType.DMA((2,)),
        pltpu.SemaphoreType.DMA((2,)),
        pltpu.SemaphoreType.DMA((ITERS, 2)),
        pltpu.SemaphoreType.DMA((ITERS, 2)),
    ]
    return pl.pallas_call(
        functools.partial(kernel_body, n, radius),
        out_shape=jax.ShapeDtypeStruct((planes, height, width), F32),
        in_specs=[pl.BlockSpec(memory_space=pltpu.VMEM)] * 2,
        out_specs=pl.BlockSpec(memory_space=pltpu.VMEM),
        scratch_shapes=scratch,
        compiler_params=pltpu.CompilerParams(
            collective_id=0, has_side_effects=True, vmem_limit_bytes=56 * 1024 * 1024
        ),
    )(raw_views, taps)


def solution(mesh):
    return jax.shard_map(
        functools.partial(local, mesh.shape["tile"]),
        mesh=mesh,
        in_specs=(P(None, ("blocks", "tile"), None, None), P()),
        out_specs=P(("blocks", "tile"), None, None),
        check_vma=False,
    )
```

profile of v0, /device:TPU:1, one launch (start us, length us, event | category | flops | bytes accessed | tf_op | source)
XLA Modules:
  0.0 88.9 jit_solution(7524337647822939298)
XLA Ops:
  0.0 0.7 convert_bitcast_fusion
  0.8 0.6 pad.4.taps
  1.4 85.7 %shard_map.28 = f32[32,32,128]{2,1,0:T(8,128)} custom-call(bf16[8,32,32,128]{3,2,1,0:T(8,128)(2,1)} %raw_in.1, bf16[48,128]{1,0:T(8,128)(2,1)} %pad.4.taps), custom_call_target="tpu_custom_call" | custom-call | tf_op jit(solution)/shard_map/pallas_call | solution.py:351
  87.1 1.9 %copy.5 = f32[32,32,128]{2,1,0:T(8,128)} copy(f32[32,32,128]{2,1,0:T(8,128)} %shard_map.28) | data formatting | bytes 1048576
  (1 shorter events, 0.0 us)
where the time goes:
time: 89.2 us; the launch traced here: 88.9 us
  Pallas kernels  85.7 us (96%)
  local copies, waits for them, and re-layouts  2.49 us (3%)
    pallas_call x1, Pallas kernels, local(): pl.pallas_call(functools.partial(kernel_body, n, radius), out_shape=jax.S...  85.7 us
    unnamed x1, local copies, waits for them, and re-layouts  1.87 us

commit v1 on v0

v1 whole, which is shorter than its diff:
```python
import functools

import jax
import jax.numpy as jnp
from jax import lax
from jax.experimental import pallas as pl
from jax.experimental.pallas import tpu as pltpu
from jax.sharding import PartitionSpec as P

ITERS = 2
SUB = 8
HALO = 16
F32 = jnp.float32
BF16 = jnp.bfloat16
MESH = pl.DeviceIdType.MESH


def dot(a, b):
    return jnp.dot(a, b, preferred_element_type=F32)


def kernel_body(
    n, radius, raw_in, taps_in, out, taps, raw, ext, est, fac, zin, zin2, qx,
    wxf, wxb, ykf, ykb, zf, zb, brow, tot, scl,
    tot_ss, tot_rs, raw_ss, raw_rs, est_ss, est_rs,
):
    views, planes, height, width = raw_in.shape
    terms = taps_in.shape[1]
    dims = taps_in.shape[2]
    me = lax.axis_index("tile")
    prev, nxt = lax.rem(me + n - 1, n), lax.rem(me + 1, n)
    has_prev, has_next = me > 0, me < n - 1
    groups = planes // SUB
    own = planes // HALO
    wide = own + 2

    barrier = pltpu.get_barrier_semaphore()

    def greet(i, c):
        pl.semaphore_signal(
            barrier, inc=1, device_id={"tile": lax.rem(me + i, n)}, device_id_type=MESH
        )
        return c

    lax.fori_loop(1, n, greet, 0)

    pl.semaphore_wait(barrier, n - 1)

    def exchange(src_lo, dst_lo, src_hi, dst_hi, ss, rs):
        down = functools.partial(
            pltpu.make_async_remote_copy,
            src_ref=src_lo, dst_ref=dst_hi, send_sem=ss.at[0], recv_sem=rs.at[0],
            device_id={"tile": prev}, device_id_type=MESH,
        )
        up = functools.partial(
            pltpu.make_async_remote_copy,
            src_ref=src_hi, dst_ref=dst_lo, send_sem=ss.at[1], recv_sem=rs.at[1],
            device_id={"tile": nxt}, device_id_type=MESH,
        )
        return down, up

    def raw_copies(v):
        return exchange(
            raw.at[v, 1], raw.at[v, 0], raw.at[v, own], raw.at[v, own + 1],
            raw_ss.at[v], raw_rs.at[v],
        )

    def est_copies(it, k):
        return exchange(
            ext.at[it, own + k], ext.at[it, k], ext.at[it, own + k], ext.at[it, 2 * own + k],
            est_ss.at[it, k], est_rs.at[it, k],
        )

    def start_down(copies):
        @pl.when(has_prev)
        def _():
            copies[0]().start()

    def start_up(copies):
        @pl.when(has_next)
        def _():
            copies[1]().start()

    def wait_hi(copies):
        @pl.when(has_next)
        def _():
            copies[0]().wait_recv()

    def wait_lo(copies):
        @pl.when(has_prev)
        def _():
            copies[1]().wait_recv()

    def wait_sent(copies):
        @pl.when(has_prev)
        def _():
            copies[0]().wait_send()

        @pl.when(has_next)
        def _():
            copies[1]().wait_send()

    area = SUB * height
    pr = lax.broadcasted_iota(jnp.int32, (area, area), 0)
    pc = lax.broadcasted_iota(jnp.int32, (area, area), 1)
    perm = (pc == (pr % SUB) * height + pr // SUB).astype(F32).astype(BF16)
    ahead = views // 2

    def relayout(v):
        total = jnp.zeros((1, 2 * width), F32)
        for k in range(own):
            halves = [
                raw_in[v, k * HALO + h * SUB:k * HALO + (h + 1) * SUB].reshape(area, width)
                for h in range(2)
            ]
            o = dot(perm, jnp.concatenate(halves, axis=1))
            total = total + jnp.sum(o, axis=0, keepdims=True)
            o = o.reshape(height, SUB, 2 * width)
            raw[v, 1 + k] = jnp.concatenate(
                [o[:, :, :width], o[:, :, width:]], axis=1
            ).astype(BF16)
        tot[0, pl.ds(v, 1), :] = total[:, :width] + total[:, width:]

    def relayout_send(v, c):
        relayout(v)
        start_down(raw_copies(v))
        start_up(raw_copies(v))
        return c

    def relayout_only(v, c):
        relayout(v)
        return c

    lax.fori_loop(0, ahead, relayout_send, 0)
    lax.fori_loop(ahead, views, relayout_only, 0)

    def tot_copy(i):
        return pltpu.make_async_remote_copy(
            src_ref=tot.at[0], dst_ref=tot.at[i], send_sem=tot_ss.at[i], recv_sem=tot_rs.at[i],
            device_id={"tile": lax.rem(me + i, n)}, device_id_type=MESH,
        )

    def tot_start(i, c):
        tot_copy(i).start()
        return c

    def tot_wait(i, c):
        tot_copy(i).wait()
        return c

    lax.fori_loop(1, n, tot_start, 0)

    @pl.when(me == 0)
    def _():
        ext[:, 0:own] = jnp.zeros_like(ext[:, 0:own])
        raw[:, 0] = jnp.zeros_like(raw[:, 0])

    @pl.when(me == n - 1)
    def _():
        ext[:, 2 * own:] = jnp.zeros_like(ext[:, 2 * own:])
        raw[:, own + 1] = jnp.zeros_like(raw[:, own + 1])

    taps[...] = jnp.zeros_like(taps)
    for v in range(views):
        for t in range(terms):
            at = (v * terms + t) * dims
            taps[at:at + dims, 0:taps_in.shape[3]] = taps_in[v, t]
    rounded_taps = taps[...].astype(BF16)

    lanes = taps.shape[1]
    tap = lax.broadcasted_iota(jnp.int32, (lanes, lanes), 0)
    lane = lax.broadcasted_iota(jnp.int32, (lanes, lanes), 1)
    signed = jnp.where(lane < lanes // 2, lane, lane - lanes)
    far = lane - lanes
    vt = views * terms

    def place(k, wanted, keep=None):
        hit = tap == wanted
        if keep is not None:
            hit = jnp.logical_and(hit, keep)
        brow[k] = dot(rounded_taps, hit.astype(F32).astype(BF16))

    step = lane % SUB == 0
    place(0, radius - signed)
    place(1, radius + signed)
    place(2, lane // SUB + radius, step)
    place(3, lane // SUB + radius - lanes // SUB, step)
    place(4, radius - lane // SUB, step)
    place(5, radius - lane // SUB + lanes // SUB, step)
    place(6, lane - (HALO - radius))
    place(7, 2 * radius + HALO - radius - lane)

    row = tap
    near = jnp.abs(row - lane) <= radius
    after = lane >= row

    def rolled(k, i, rows):
        line = jnp.broadcast_to(brow[k, pl.ds(dims * i[0] + i[1], 1), :], (rows, lanes))
        return pltpu.roll(line, 0, 1, stride=1, stride_axis=0)

    def tables(wx, yk, z, kx, ky, kz, zrows, zcols):
        def one(v, c):
            for t in range(terms):
                i = v * terms + t
                wx[v, t * width:(t + 1) * width, :] = jnp.where(
                    near, rolled(kx, (i, 2), width), 0.0
                ).astype(BF16)
                r0 = rolled(ky, (i, 1), lanes)
                r1 = rolled(ky + 1, (i, 1), lanes)
                t0 = jnp.where(after, r0, r1).astype(BF16)
                yk[i, 0:lanes, 0:lanes] = t0
                yk[i, lanes:2 * lanes, lanes:2 * lanes] = t0
                yk[i, 0:lanes, lanes:2 * lanes] = jnp.where(after, 0.0, r0).astype(BF16)
                yk[i, lanes:2 * lanes, 0:lanes] = jnp.where(after, r1, 0.0).astype(BF16)
                z[v, t * zrows:(t + 1) * zrows, :] = rolled(kz, (i, 0), zrows)[:, :zcols].astype(BF16)
            return c

        lax.fori_loop(0, views, one, 0)

    tables(wxf, ykf, zf, 0, 2, 6, HALO, zf.shape[2])

    lax.fori_loop(1, n, tot_wait, 0)
    summed = lax.fori_loop(0, n, lambda i, a: a + tot[i], jnp.zeros(tot.shape[1:], F32))
    totals = jnp.sum(summed, axis=1, keepdims=True)
    mean = jnp.sum(totals, axis=0, keepdims=True) / views
    scl[...] = jnp.broadcast_to(mean / totals, scl.shape)

    chunk = SUB
    for k in range(own):
        def first(j, c):
            acc = jnp.zeros((chunk, HALO, width), F32)
            for v in range(views):
                s = scl[v:v + 1, :].reshape(1, 1, width)
                acc = acc + s * raw[v, 1 + k, pl.ds(j * chunk, chunk)].astype(F32)
            acc = acc / views
            for h in range(HALO // SUB):
                est[k * (HALO // SUB) + h, pl.ds(j * chunk * SUB, chunk * SUB), :] = acc[
                    :, h * SUB:(h + 1) * SUB, :
                ].reshape(chunk * SUB, width)
            ext[0, own + k, pl.ds(j * chunk, chunk)] = acc.astype(BF16)
            return c

        lax.fori_loop(0, height // chunk, first, 0)

    def send_est(it, k):
        copies = est_copies(it, k)
        if k < own // 2:
            start_down(copies)
            start_up(copies)
        else:
            start_up(copies)
            start_down(copies)

    for k in range(own):
        send_est(0, k)

    def raw_start(v, c):
        start_down(raw_copies(v))
        start_up(raw_copies(v))
        return c

    lax.fori_loop(ahead, views, raw_start, 0)
    tables(wxb, ykb, zb, 1, 4, 7, planes, zb.shape[2])

    pairs = height // 2

    def yx(yk, wx, z, v, first, step):
        ys = []
        for t in range(terms):
            i = first + t * step
            rhs = jnp.concatenate([z[i], z[i + 1]], axis=1)
            ys.append(dot(yk[v * terms + t], rhs).astype(BF16))
        lhs = jnp.concatenate(
            [
                jnp.concatenate([y[:, h * width:(h + 1) * width] for y in ys], axis=1)
                for h in range(2)
            ],
            axis=0,
        )
        res = dot(lhs, wx[v])
        return [res[h * area:(h + 1) * area] for h in range(2)]

    order = list(range(own, 0, -1)) + [own + 1, 0]
    for it in range(ITERS):
        def forward(gp):
            def zforward(p, c):
                cols = [
                    jnp.concatenate(
                        [ext[it, own + gp - 2 + d, 2 * p + h] for d in range(3)], axis=0
                    )
                    for h in range(2)
                ]
                rhs = jnp.concatenate(cols, axis=1)
                r = dot(zf[...].reshape(-1, zf.shape[2]), rhs)
                r = r.reshape(vt * 2, SUB, 2 * width)
                r = jnp.concatenate([r[:, :, :width], r[:, :, width:]], axis=1)
                at = pl.ds(pl.multiple_of(p * 2 * SUB, 2 * SUB), 2 * SUB)
                zin[:, at, :] = r.astype(BF16)
                return c

            lax.fori_loop(0, pairs, zforward, 0, unroll=2)

            def one(v, c):
                s = scl[pl.ds(v, 1), :].reshape(1, 1, width)
                if it == 0 and gp == 0:
                    wait_lo(raw_copies(v))
                if it == 0 and gp == wide - 1:
                    wait_hi(raw_copies(v))
                res = yx(ykf, wxf, zin, v, v * terms * 2, 2)
                b = jnp.concatenate([x.reshape(height, SUB, width) for x in res], axis=1)
                q = s * raw[v, gp].astype(F32) / b
                if gp == 0:
                    q = jnp.where(has_prev, q, 0.0)
                if gp == wide - 1:
                    q = jnp.where(has_next, q, 0.0)
                qx[v, gp] = q.astype(BF16)
                return c

            lax.fori_loop(0, views, one, 0, unroll=1 if it == 0 and gp in (0, wide - 1) else 4)

        for gp in order:
            if gp == own:
                wait_hi(est_copies(it, 0))
            if gp == 1:
                wait_lo(est_copies(it, own - 1))
            if gp == wide - 1:
                for k in range(1, own):
                    wait_hi(est_copies(it, k))
            if gp == 0:
                for k in range(own - 1):
                    wait_lo(est_copies(it, k))
            forward(gp)

        def zbackward(v, c):
            for p in range(pairs):
                cols = [
                    jnp.concatenate([qx[v, g, 2 * p + h] for g in range(wide)], axis=0)
                    for h in range(2)
                ]
                r = dot(zb[v], jnp.concatenate(cols, axis=1))
                r = r.reshape(terms * groups, SUB, 2 * width)
                r = jnp.concatenate([r[:, :, :width], r[:, :, width:]], axis=1)
                zin2[pl.ds(v * terms * groups, terms * groups), p * 2 * SUB:(p + 1) * 2 * SUB, :] = (
                    r.astype(BF16)
                )
            return c

        lax.fori_loop(0, views, zbackward, 0)
        fac[...] = jnp.ones_like(fac)

        for k in range(own):
            def backward(v, c):
                res = yx(ykb, wxb, zin2, v, v * terms * groups + 2 * k, groups)
                for h in range(2):
                    fac[2 * k + h] = fac[2 * k + h] * res[h]
                return c

            lax.fori_loop(0, views, backward, 0, unroll=4)
            parts = []
            for h in range(2):
                g = 2 * k + h
                new = est[g] * fac[g]
                est[g] = new
                parts.append(new.reshape(height, SUB, width))
            if it + 1 < ITERS:
                ext[it + 1, own + k] = jnp.concatenate(parts, axis=1).astype(BF16)
                send_est(it + 1, k)

    for g in range(groups):
        for z in range(SUB):
            out[g * SUB + z] = est[g, pl.ds(z, height, stride=SUB), :]

    def raw_sent(v, c):
        wait_sent(raw_copies(v))
        return c

    lax.fori_loop(0, views, raw_sent, 0)
    for it in range(ITERS):
        for k in range(own):
            wait_sent(est_copies(it, k))


def local(n, raw_views, spread_taps):
    views, planes, height, width = raw_views.shape
    terms, tap_count = spread_taps.shape[1], spread_taps.shape[3]
    radius = (tap_count - 1) // 2
    vt = views * terms
    own = planes // HALO
    wide = own + 2
    area = SUB * height
    scratch = [
        pltpu.VMEM((3 * vt, width), F32),
        pltpu.VMEM((views, wide, height, HALO, width), BF16),
        pltpu.VMEM((ITERS, 3 * own, height, HALO, width), BF16),
        pltpu.VMEM((planes // SUB, area, width), F32),
        pltpu.VMEM((planes // SUB, area, width), F32),
        pltpu.VMEM((vt * HALO // SUB, area, width), BF16),
        pltpu.VMEM((vt * planes // SUB, area, width), BF16),
        pltpu.VMEM((views, wide, height, HALO, width), BF16),
        pltpu.VMEM((views, terms * width, width), BF16),
        pltpu.VMEM((views, terms * width, width), BF16),
        pltpu.VMEM((vt, area, area), BF16),
        pltpu.VMEM((vt, area, area), BF16),
        pltpu.VMEM((views, terms * HALO, 3 * HALO), BF16),
        pltpu.VMEM((views, terms * planes, wide * HALO), BF16),
        pltpu.VMEM((8, 3 * vt, width), F32),
        pltpu.VMEM((n, views, width), F32),
        pltpu.VMEM((views, width), F32),
        pltpu.SemaphoreType.DMA((n,)),
        pltpu.SemaphoreType.DMA((n,)),
        pltpu.SemaphoreType.DMA((views, 2)),
        pltpu.SemaphoreType.DMA((views, 2)),
        pltpu.SemaphoreType.DMA((ITERS, own, 2)),
        pltpu.SemaphoreType.DMA((ITERS, own, 2)),
    ]
    return pl.pallas_call(
        functools.partial(kernel_body, n, radius),
        out_shape=jax.ShapeDtypeStruct((planes, height, width), F32),
        in_specs=[pl.BlockSpec(memory_space=pltpu.VMEM)] * 2,
        out_specs=pl.BlockSpec(memory_space=pltpu.VMEM),
        scratch_shapes=scratch,
        compiler_params=pltpu.CompilerParams(
            collective_id=0, has_side_effects=True, vmem_limit_bytes=56 * 1024 * 1024
        ),
    )(raw_views, spread_taps)


def solution(mesh):
    return jax.shard_map(
        functools.partial(local, mesh.shape["tile"]),
        mesh=mesh,
        in_specs=(P(None, ("blocks", "tile"), None, None), P()),
        out_specs=P(("blocks", "tile"), None, None),
        check_vma=False,
    )
```

time: 89.2 us -> 81.6 us (0.915)
  Pallas kernels: 85.7 us -> 78 us
    pallas_call x1, Pallas kernels: 85.7 us -> 78 us  [local(): pl.pallas_call(functools.partial(kernel_body, n, radius), out_shape=jax.S...]
    unnamed x1 -> x2, local copies, waits for them, and re-layouts: 1.87 us -> 3.23 us
where the time goes in v1:
time: 81.6 us; the launch traced here: 81.2 us
  Pallas kernels  78 us (96%)
  local copies, waits for them, and re-layouts  3.23 us (4%)
    pallas_call x1, Pallas kernels, local(): pl.pallas_call(functools.partial(kernel_body, n, radius), out_shape=jax.S...  78 us
    unnamed x2, local copies, waits for them, and re-layouts  3.23 us

profile of v1, /device:TPU:1, one launch (start us, length us, event | category | flops | bytes accessed | tf_op | source)
XLA Modules:
  0.0 81.2 jit_solution(12725695031482317408)
XLA Ops:
  0.0 1.4 %copy.3.taps_in = f32[8,2,3,31]{3,2,1,0:T(4,128)} copy(f32[8,2,3,31]{3,1,2,0:T(2,128)} %param.3) | data formatting | bytes 11904 | tf_op args[1]
  1.4 78.0 %shard_map.28 = f32[32,32,128]{2,1,0:T(8,128)} custom-call(bf16[8,32,32,128]{3,2,1,0:T(8,128)(2,1)} %raw_in.1, f32[8,2,3,31]{3,2,1,0:T(4,128)} %copy.3.taps_in), custom_call_target="tpu_custom_call" | custom-call | tf_op jit(solution)/shard_map/pallas_call | solution.py:416
  79.3 1.9 %copy.5 = f32[32,32,128]{2,1,0:T(8,128)} copy(f32[32,32,128]{2,1,0:T(8,128)} %shard_map.28) | data formatting | bytes 1048576
